TPU v7x, 32 devices: a whole 2x2x4 slice. The times are simulated.
32 devices in a mesh: ctx: 4 (over y, x), exp: 8 (over z, core).
Axes of the slice: x: 2, y: 2, z: 4, core: 2. Of those that a mesh axis runs over, the one named last changes fastest.
Arguments:
- tokens: bfloat16 [1024, 7168], P('exp', 'ctx'), may hold values from -6 to 6
- cotangent: bfloat16 [1024, 7168], P('exp', 'ctx'), may hold values from -6 to 6
- routes: int32 [1024, 8], P('exp'), may hold values from 0 to 255, all different within a row; in each aligned block of 128 rows (0 to 127, 128 to 255, ...) at most 6 rows name the same one
- gate_weights: float32 [1024, 8], P('exp'), may hold values from 0.1 to 0.7
- w_gate: bfloat16 [8, 7168, 1024], P('exp', 'ctx'), may hold values from -0.0625 to 0.0625
- w_up: bfloat16 [8, 7168, 1024], P('exp', 'ctx'), may hold values from -0.0625 to 0.0625
- w_down: bfloat16 [8, 1024, 7168], P('exp', None, 'ctx'), may hold values from -0.1875 to 0.1875
Outputs:
- combined: bfloat16 [1024, 7168], P('exp', 'ctx')
- d_tokens: bfloat16 [1024, 7168], P('exp', 'ctx')
- d_gate: bfloat16 [8, 7168, 1024], P('exp', 'ctx')
- d_up: bfloat16 [8, 7168, 1024], P('exp', 'ctx')
- d_down: bfloat16 [8, 1024, 7168], P('exp', None, 'ctx')
Inputs may be any that keep to these rules, and one draw needn't show every extreme that they name: The 8 routes of a token are distinct. Within each aligned block of 128 tokens no expert is named by more than 6 tokens, a bound that some block reaches.
All inputs are finite; a program needn't handle non-finite values.
Results may differ from a plain program's by a relative error of at most 0.0066.
Values may be sent and summed in bfloat16 or wider, within the bound.
A program may use at most 64 MiB of HBM per device.

v0:
```python
import jax
import jax.numpy as jnp
from jax import lax
from jax.sharding import PartitionSpec as P

CAP = 6


def contract_last(left, right):
    return lax.dot_general(
        left, right, (((1,), (1,)), ((), ())), preferred_element_type=jnp.float32
    )


def contract_first(left, right):
    return lax.dot_general(
        left, right, (((0,), (0,)), ((), ())), preferred_element_type=jnp.float32
    )


def forward_share(gate_sum, up_sum):
    sigmoid_gate = jax.nn.sigmoid(gate_sum)
    return (gate_sum * sigmoid_gate * up_sum).astype(jnp.bfloat16)


def backward_share(gate_sum, up_sum, back_sum):
    sigmoid_gate = jax.nn.sigmoid(gate_sum)
    activated = gate_sum * sigmoid_gate
    d_gate_act = (
        back_sum * up_sum * sigmoid_gate * (1.0 + gate_sum * (1.0 - sigmoid_gate))
    ).astype(jnp.bfloat16)
    d_up_act = (back_sum * activated).astype(jnp.bfloat16)
    return (d_gate_act, d_up_act)


def shards(tokens, cotangent, routes, gate_weights, w_gate, w_up, w_down):
    experts = lax.axis_size("exp")
    tok_count, picks = routes.shape
    feature_width = tokens.shape[1]
    slot_total = experts * CAP
    flat_ids = routes.reshape(-1)
    columns = jnp.arange(experts, dtype=jnp.int32)
    onehot = (flat_ids[:, None] == columns[None, :]).astype(jnp.int32)
    earlier = jnp.cumsum(onehot, axis=0) - onehot
    slot_index = jnp.sum(onehot * earlier, axis=1)
    target = jnp.where(flat_ids < experts, flat_ids * CAP + slot_index, -1).reshape(
        tok_count, picks
    )
    places = jnp.arange(slot_total, dtype=jnp.int32)
    matches = target[None, :, :] == places[:, None, None]
    select = jnp.any(matches, axis=2).astype(jnp.bfloat16)
    rounded = gate_weights.astype(jnp.bfloat16).astype(jnp.float32)
    weighting = jnp.sum(jnp.where(matches, rounded[None, :, :], 0.0), axis=2).astype(jnp.bfloat16)
    send_rows = jnp.dot(select, tokens, preferred_element_type=jnp.float32).astype(jnp.bfloat16)
    send_grads = jnp.dot(weighting, cotangent, preferred_element_type=jnp.float32).astype(
        jnp.bfloat16
    )
    got_rows, got_grads = (
        lax.all_to_all(
            send_rows.reshape(experts, CAP, feature_width),
            "exp",
            split_axis=0,
            concat_axis=0,
            tiled=True,
        ),
        lax.all_to_all(
            send_grads.reshape(experts, CAP, feature_width),
            "exp",
            split_axis=0,
            concat_axis=0,
            tiled=True,
        ),
    )
    inputs = got_rows.reshape(slot_total, feature_width)
    slot_grads = got_grads.reshape(slot_total, feature_width)
    gate_matrix = w_gate[0]
    up_matrix = w_up[0]
    down_matrix = w_down[0]
    gate_part = jnp.dot(inputs, gate_matrix, preferred_element_type=jnp.float32)
    up_part = jnp.dot(inputs, up_matrix, preferred_element_type=jnp.float32)
    gate_sum, up_sum = (
        lax.psum_scatter(gate_part, "ctx", scatter_dimension=0, tiled=True),
        lax.psum_scatter(up_part, "ctx", scatter_dimension=0, tiled=True),
    )
    full_hidden = lax.all_gather(forward_share(gate_sum, up_sum), "ctx", axis=0, tiled=True)
    expert_out = jnp.dot(full_hidden, down_matrix, preferred_element_type=jnp.float32).astype(
        jnp.bfloat16
    )
    back_part = contract_last(slot_grads, down_matrix)
    back_sum = lax.psum_scatter(back_part, "ctx", scatter_dimension=0, tiled=True)
    d_gate_act, d_up_act = backward_share(gate_sum, up_sum, back_sum)
    full_dgate, full_dup = (
        lax.all_gather(d_gate_act, "ctx", axis=0, tiled=True),
        lax.all_gather(d_up_act, "ctx", axis=0, tiled=True),
    )
    d_down = contract_first(full_hidden, slot_grads).astype(jnp.bfloat16)
    d_gate = contract_first(inputs, full_dgate).astype(jnp.bfloat16)
    d_up = contract_first(inputs, full_dup).astype(jnp.bfloat16)
    d_inputs = (contract_last(full_dgate, gate_matrix) + contract_last(full_dup, up_matrix)).astype(
        jnp.bfloat16
    )
    back_out, back_grads = (
        lax.all_to_all(
            expert_out.reshape(experts, CAP, feature_width),
            "exp",
            split_axis=0,
            concat_axis=0,
            tiled=True,
        ),
        lax.all_to_all(
            d_inputs.reshape(experts, CAP, feature_width),
            "exp",
            split_axis=0,
            concat_axis=0,
            tiled=True,
        ),
    )
    combined = contract_first(weighting, back_out.reshape(slot_total, feature_width)).astype(
        jnp.bfloat16
    )
    d_tokens = contract_first(select, back_grads.reshape(slot_total, feature_width)).astype(
        jnp.bfloat16
    )
    return (combined, d_tokens, d_gate[None], d_up[None], d_down[None])


def solution(mesh):
    in_specs = (
        P("exp", "ctx"),
        P("exp", "ctx"),
        P("exp", None),
        P("exp", None),
        P("exp", "ctx", None),
        P("exp", "ctx", None),
        P("exp", None, "ctx"),
    )
    out_specs = (
        P("exp", "ctx"),
        P("exp", "ctx"),
        P("exp", "ctx", None),
        P("exp", "ctx", None),
        P("exp", None, "ctx"),
    )
    return jax.shard_map(shards, mesh=mesh, in_specs=in_specs, out_specs=out_specs, check_vma=False)
```

profile of v0, /device:TPU:0, one launch (start us, length us, event | category | flops | bytes accessed | tf_op | source)
XLA Modules:
  0.0 126.3 jit_solution(7037325629726876075)
XLA Ops:
  0.6 0.8 copy.35
  1.7 2.3 %reduce-window.6 = s32[8,8,128]{2,1,0:T(8,128)S(1)} reduce-window(s32[8,8,128]{2,1,0:T(8,128)S(1)} %fusion.34, s32[]{:T(128)} %constant.4.clone.1), window={size=1x1x128 pad=0_0x0_0x127_0}, to_apply=%region_0.0 | reduce-window | flops 1040384 | bytes 65540 | tf_op jit(solution)/shard_map/reduce-window
  5.7 0.7 reshape.62
  6.4 6.3 %all-to-all-start = ((bf16[8,6,1792]{2,1,0:T(8,128)(2,1)}), bf16[8,6,1792]{2,1,0:T(8,128)(2,1)S(1)}, u32[]{:S(2)}, u32[]{:S(2)}) async-start(bf16[8,6,1792]{2,1,0:T(8,128)(2,1)} %reshape.62), calls=%async_computation | async-start | bytes 458752 | tf_op jit(solution)/shard_map/all_to_all | solution.py:59
  13.5 1.2 convolution_convert_fusion.5
  14.7 0.8 reshape.66
  15.5 6.3 %all-to-all-done = bf16[8,6,1792]{2,1,0:T(8,128)(2,1)S(1)} async-done(((bf16[8,6,1792]{2,1,0:T(8,128)(2,1)}), bf16[8,6,1792]{2,1,0:T(8,128)(2,1)S(1)}, u32[]{:S(2)}, u32[]{:S(2)}) %all-to-all-start) | async-done | bytes 172064 | tf_op jit(solution)/shard_map/all_to_all | solution.py:59
  21.8 3.4 %all-to-all-start.2 = ((bf16[8,6,1792]{2,1,0:T(8,128)(2,1)}), bf16[8,6,1792]{2,1,0:T(8,128)(2,1)S(1)}, u32[]{:S(2)}, u32[]{:S(2)}) async-start(bf16[8,6,1792]{2,1,0:T(8,128)(2,1)} %reshape.66), calls=%async_computation.2 | async-start | bytes 458752 | tf_op jit(solution)/shard_map/all_to_all | solution.py:66
  25.3 2.9 %fusion.13 = f32[48,1024]{1,0:T(8,128)S(1)} fusion(bf16[48,1792]{1,0:T(8,128)(2,1)S(1)} %reshape.63, bf16[1,1792,1024]{2,1,0:T(8,128)(2,1)} %param.11), kind=kOutput, calls=%fused_computation.13 | convolution fusion | flops 176160768 | bytes 4038656 | tf_op jit(solution)/shard_map/dot_general | solution.py:79
  28.4 0.7 fusion.9
  29.2 5.0 %all-to-all-done.2 = bf16[8,6,1792]{2,1,0:T(8,128)(2,1)S(1)} async-done(((bf16[8,6,1792]{2,1,0:T(8,128)(2,1)}), bf16[8,6,1792]{2,1,0:T(8,128)(2,1)S(1)}, u32[]{:S(2)}, u32[]{:S(2)}) %all-to-all-start.2) | async-done | bytes 172064 | tf_op jit(solution)/shard_map/all_to_all | solution.py:66
  34.2 3.2 %fusion.3 = f32[48,1024]{1,0:T(8,128)S(1)} fusion(bf16[48,1792]{1,0:T(8,128)(2,1)S(1)} %reshape.67, bf16[1,1024,1792]{2,1,0:T(8,128)(2,1)} %param.13), kind=kOutput, calls=%fused_computation.3 | convolution fusion | flops 176160768 | bytes 4038656 | tf_op jit(solution)/shard_map/dot_general | solution.py:10
  37.4 19.9 %fusion.38 = (f32[16,1024]{1,0:T(8,128)S(1)}, f32[16,1024]{1,0:T(8,128)S(1)}, f32[16,1024]{1,0:T(8,128)S(1)}) fusion(f32[48,1024]{1,0:T(8,128)S(1)} %fusion.9, f32[48,1024]{1,0:T(8,128)S(1)} %fusion.13, f32[48,1024]{1,0:T(8,128)S(1)} %fusion.3), kind=kCustom, calls=%all-reduce-scatter.3 | all-reduce-scatter fusion | flops 196609 | bytes 786944
  57.3 1.5 %collective-permute-start.2 = (f32[12,1024]{1,0:T(8,128)S(1)}, f32[12,1024]{1,0:T(8,128)S(1)}, u32[]{:S(2)}, u32[]{:S(2)}) collective-permute-start(f32[12,1024]{1,0:T(8,128)S(1)} %slice.11), channel_id=1, source_target_pairs={{0,8},{8,16},{16,24},{1,9},{9,17},{17,25},{2,10},{10,18},{18,26},{... | collective-permute-start | bytes 147464
  58.9 4.3 %collective-permute-start.1 = (f32[12,1024]{1,0:T(8,128)S(1)}, f32[12,1024]{1,0:T(8,128)S(1)}, u32[]{:S(2)}, u32[]{:S(2)}) collective-permute-start(f32[12,1024]{1,0:T(8,128)S(1)} %slice.10), channel_id=1, source_target_pairs={{0,8},{8,16},{16,24},{1,9},{9,17},{17,25},{2,10},{10,18},{18,26},{... | collective-permute-start | bytes 147464
  63.2 1.9 %collective-permute-start = (f32[12,1024]{1,0:T(8,128)S(1)}, f32[12,1024]{1,0:T(8,128)S(1)}, u32[]{:S(2)}, u32[]{:S(2)}) collective-permute-start(f32[12,1024]{1,0:T(8,128)S(1)} %slice.9), channel_id=1, source_target_pairs={{0,8},{8,16},{16,24},{1,9},{9,17},{17,25},{2,10},{10,18},{18,26},{... | collective-permute-start | bytes 147464
  67.2 9.5 %all-gather = bf16[4,12,1024]{2,1,0:T(8,128)(2,1)S(1)} all-gather(bf16[1,12,1024]{2,1,0:T(8,128)(2,1)S(1)} %get-tuple-element.13), channel_id=1, replica_groups=mesh['ctx'=4,'exp'=8] {'ctx'}, dimensions={0}, use_global_device_ids=true | all-gather | bytes 122880 | tf_op jit(solution)/shard_map/all_gather | solution.py:85
  76.7 6.9 %all-gather.1 = bf16[4,12,1024]{2,1,0:T(8,128)(2,1)S(1)} all-gather(bf16[1,12,1024]{2,1,0:T(8,128)(2,1)S(1)} %get-tuple-element.11), channel_id=1, replica_groups=mesh['ctx'=4,'exp'=8] {'ctx'}, dimensions={0}, use_global_device_ids=true | all-gather | bytes 122880 | tf_op jit(solution)/shard_map/all_gather | solution.py:93
  83.7 9.0 %all-gather.2 = bf16[4,12,1024]{2,1,0:T(8,128)(2,1)S(1)} all-gather(bf16[1,12,1024]{2,1,0:T(8,128)(2,1)S(1)} %get-tuple-element.12), channel_id=1, replica_groups=mesh['ctx'=4,'exp'=8] {'ctx'}, dimensions={0}, use_global_device_ids=true | all-gather | bytes 122880 | tf_op jit(solution)/shard_map/all_gather | solution.py:94
  92.7 3.4 %fusion.7 = f32[48,1792]{1,0:T(8,128)S(1)} fusion(bf16[48,1024]{1,0:T(8,128)(2,1)S(1)} %reshape.75, bf16[1,1792,1024]{2,1,0:T(8,128)(2,1)} %param.12), kind=kOutput, calls=%fused_computation.7 | convolution fusion | flops 176160768 | bytes 4112384 | tf_op jit(solution)/shard_map/dot_general | solution.py:10
  96.2 1.2 fusion.21
  97.4 0.7 reshape.68
  98.1 3.4 %all-to-all-start.3 = ((bf16[8,6,1792]{2,1,0:T(8,128)(2,1)}), bf16[8,6,1792]{2,1,0:T(8,128)(2,1)S(1)}, u32[]{:S(2)}, u32[]{:S(2)}) async-start(bf16[8,6,1792]{2,1,0:T(8,128)(2,1)} %reshape.68), calls=%async_computation.3 | async-start | bytes 458752 | tf_op jit(solution)/shard_map/all_to_all | solution.py:110
  101.6 2.8 %fusion.24 = bf16[48,1792]{1,0:T(8,128)(2,1)S(1)} fusion(bf16[48,1024]{1,0:T(8,128)(2,1)S(1)} %reshape.71, bf16[1,1024,1792]{2,1,0:T(8,128)(2,1)} %param.13), kind=kOutput, calls=%fused_computation.22 | convolution fusion | flops 176246784 | bytes 3940352 | tf_op jit(solution)/shard_map/dot_general | solution.py:86
  104.3 0.7 reshape.64
  105.1 3.0 %fusion.17 = bf16[1,1024,1792]{2,1,0:T(8,128)(2,1)} fusion(bf16[48,1024]{1,0:T(8,128)(2,1)S(1)} %reshape.71, bf16[48,1792]{1,0:T(8,128)(2,1)S(1)} %reshape.67), kind=kOutput, calls=%fused_computation.17 | convolution fusion | flops 177995776 | bytes 3940352 | tf_op jit(solution)/shard_map/dot_general | solution.py:16
  108.1 3.0 %fusion.15 = bf16[1,1792,1024]{2,1,0:T(8,128)(2,1)} fusion(bf16[48,1792]{1,0:T(8,128)(2,1)S(1)} %reshape.63, bf16[48,1024]{1,0:T(8,128)(2,1)S(1)} %reshape.73), kind=kOutput, calls=%fused_computation.15 | convolution fusion | flops 177995776 | bytes 3940352 | tf_op jit(solution)/shard_map/dot_general | solution.py:16
  111.1 5.0 %all-to-all-start.1 = ((bf16[8,6,1792]{2,1,0:T(8,128)(2,1)}), bf16[8,6,1792]{2,1,0:T(8,128)(2,1)S(1)}, u32[]{:S(2)}, u32[]{:S(2)}) async-start(bf16[8,6,1792]{2,1,0:T(8,128)(2,1)} %reshape.64), calls=%async_computation.1 | async-start | bytes 458752 | tf_op jit(solution)/shard_map/all_to_all | solution.py:103
  116.1 3.0 %fusion.16 = bf16[1,1792,1024]{2,1,0:T(8,128)(2,1)} fusion(bf16[48,1792]{1,0:T(8,128)(2,1)S(1)} %reshape.63, bf16[48,1024]{1,0:T(8,128)(2,1)S(1)} %reshape.75), kind=kOutput, calls=%fused_computation.16 | convolution fusion | flops 177995776 | bytes 3940352 | tf_op jit(solution)/shard_map/dot_general | solution.py:16
  119.1 1.1 convolution_convert_fusion.3
  120.2 4.9 %all-to-all-done.1 = bf16[8,6,1792]{2,1,0:T(8,128)(2,1)S(1)} async-done(((bf16[8,6,1792]{2,1,0:T(8,128)(2,1)}), bf16[8,6,1792]{2,1,0:T(8,128)(2,1)S(1)}, u32[]{:S(2)}, u32[]{:S(2)}) %all-to-all-start.1) | async-done | bytes 172064 | tf_op jit(solution)/shard_map/all_to_all | solution.py:103
  125.2 1.1 convolution_convert_fusion.4
  (41 shorter events, 4.6 us)
Async XLA Ops:
  0.6 4.8 %copy-start = (bf16[128,1792]{1,0:T(8,128)(2,1)S(1)}, bf16[128,1792]{1,0:T(8,128)(2,1)}, u32[]{:S(2)}) copy-start(bf16[128,1792]{1,0:T(8,128)(2,1)} %param.7) | copy-start | bytes 1376260
  6.4 15.4 %all-to-all-start = ((bf16[8,6,1792]{2,1,0:T(8,128)(2,1)}), bf16[8,6,1792]{2,1,0:T(8,128)(2,1)S(1)}, u32[]{:S(2)}, u32[]{:S(2)}) async-start(bf16[8,6,1792]{2,1,0:T(8,128)(2,1)} %reshape.62), calls=%async_computation | async-start | bytes 458752 | tf_op jit(solution)/shard_map/all_to_all | solution.py:59
  21.8 12.4 %all-to-all-start.2 = ((bf16[8,6,1792]{2,1,0:T(8,128)(2,1)}), bf16[8,6,1792]{2,1,0:T(8,128)(2,1)S(1)}, u32[]{:S(2)}, u32[]{:S(2)}) async-start(bf16[8,6,1792]{2,1,0:T(8,128)(2,1)} %reshape.66), calls=%async_computation.2 | async-start | bytes 458752 | tf_op jit(solution)/shard_map/all_to_all | solution.py:66
  25.2 3.1 %copy-start.1 = (bf16[1,1792,1024]{2,1,0:T(8,128)(2,1)S(1)}, bf16[1,1792,1024]{2,1,0:T(8,128)(2,1)}, u32[]{:S(2)}) copy-start(bf16[1,1792,1024]{2,1,0:T(8,128)(2,1)} %param.12) | copy-start | bytes 11010052
  29.1 35.9 %copy-start.3 = (u32[32]{0:T(128)S(1)}, u32[32]{0:T(128)}, u32[]{:S(2)}) copy-start(u32[32]{0:T(128)} %constant.23) | copy-start | bytes 388
  57.3 9.0 %collective-permute-start.2 = (f32[12,1024]{1,0:T(8,128)S(1)}, f32[12,1024]{1,0:T(8,128)S(1)}, u32[]{:S(2)}, u32[]{:S(2)}) collective-permute-start(f32[12,1024]{1,0:T(8,128)S(1)} %slice.11), channel_id=1, source_target_pairs={{0,8},{8,16},{16,24},{1,9},{9,17},{17,25},{2,10},{10,18},{18,26},{... | collective-permute-start | bytes 147464
  58.9 7.7 %collective-permute-start.1 = (f32[12,1024]{1,0:T(8,128)S(1)}, f32[12,1024]{1,0:T(8,128)S(1)}, u32[]{:S(2)}, u32[]{:S(2)}) collective-permute-start(f32[12,1024]{1,0:T(8,128)S(1)} %slice.10), channel_id=1, source_target_pairs={{0,8},{8,16},{16,24},{1,9},{9,17},{17,25},{2,10},{10,18},{18,26},{... | collective-permute-start | bytes 147464
  63.2 3.8 %collective-permute-start = (f32[12,1024]{1,0:T(8,128)S(1)}, f32[12,1024]{1,0:T(8,128)S(1)}, u32[]{:S(2)}, u32[]{:S(2)}) collective-permute-start(f32[12,1024]{1,0:T(8,128)S(1)} %slice.9), channel_id=1, source_target_pairs={{0,8},{8,16},{16,24},{1,9},{9,17},{17,25},{2,10},{10,18},{18,26},{... | collective-permute-start | bytes 147464
  92.7 3.4 %copy-start.2 = (bf16[1,1792,1024]{2,1,0:T(8,128)(2,1)S(1)}, bf16[1,1792,1024]{2,1,0:T(8,128)(2,1)}, u32[]{:S(2)}) copy-start(bf16[1,1792,1024]{2,1,0:T(8,128)(2,1)} %param.11) | copy-start | bytes 11010052
  98.1 12.9 %all-to-all-start.3 = ((bf16[8,6,1792]{2,1,0:T(8,128)(2,1)}), bf16[8,6,1792]{2,1,0:T(8,128)(2,1)S(1)}, u32[]{:S(2)}, u32[]{:S(2)}) async-start(bf16[8,6,1792]{2,1,0:T(8,128)(2,1)} %reshape.68), calls=%async_computation.3 | async-start | bytes 458752 | tf_op jit(solution)/shard_map/all_to_all | solution.py:110
  111.1 14.1 %all-to-all-start.1 = ((bf16[8,6,1792]{2,1,0:T(8,128)(2,1)}), bf16[8,6,1792]{2,1,0:T(8,128)(2,1)S(1)}, u32[]{:S(2)}, u32[]{:S(2)}) async-start(bf16[8,6,1792]{2,1,0:T(8,128)(2,1)} %reshape.64), calls=%async_computation.1 | async-start | bytes 458752 | tf_op jit(solution)/shard_map/all_to_all | solution.py:103
where the time goes:
time: 127 us; the launch traced here: 126 us
  blocking collectives  45.3 us (36%)
  matrix products  26.8 us (21%)
  starting transfers between devices  25.9 us (20%)
  waiting for transfers between devices  16.5 us (13%)
  local copies, waits for them, and re-layouts  6.08 us (5%)
  other arithmetic  4.15 us (3%)
  between operations  1.59 us (1%)
    unnamed x1, blocking collectives  19.9 us
    dot_general x5, matrix products, contract_first(): lax.dot_general(left, right, (((0,), (0,)), ((), ())), preferred_element_...  11.1 us
    all_gather x1, blocking collectives, shards(): lax.all_gather(forward_share(gate_sum, up_sum), 'ctx', axis=0, tiled=True)  9.5 us
    all_gather x1, blocking collectives, shards(): lax.all_gather(d_up_act, 'ctx', axis=0, tiled=True)  8.99 us
    dot_general x3, matrix products, contract_last(): lax.dot_general(left, right, (((1,), (1,)), ((), ())), preferred_element_...  7.83 us
    unnamed x3, starting transfers between devices  7.7 us
    all_gather x1, blocking collectives, shards(): lax.all_gather(d_gate_act, 'ctx', axis=0, tiled=True)  6.94 us
    all_to_all x1, starting transfers between devices, shards(): lax.all_to_all(send_rows.reshape(experts, CAP, feature_width), 'exp', spl...  6.33 us
  transfers between devices with their start and end apart: 7, of which 4 were waited for; matrix products, arithmetic and copies ran while one was open for 17% of the time, Pallas kernels for 0%

commit v1 on v0

v1 whole, which is shorter than its diff:
```python
import functools

import jax
import jax.numpy as jnp
from jax import lax
from jax.experimental import pallas as pl
from jax.experimental.pallas import tpu as pltpu
from jax.sharding import PartitionSpec as P

HALF = 8
PAIR = 2 * HALF


def dot(left, right, left_dim=1, right_dim=0):
    return lax.dot_general(
        left,
        right,
        (((left_dim,), (right_dim,)), ((), ())),
        preferred_element_type=jnp.float32,
    )


def pieces(width):
    if width % 256 or width < 512:
        return [(0, width)]
    first = (width // 256 + 1) // 2 * 256
    return [(0, first), (first, width - first)]


def selections(routes, gates, count):
    tok_count, picks = routes.shape
    shape = (tok_count, count * PAIR)
    lane = lax.broadcasted_iota(jnp.int32, shape, 1)
    expert = lane // PAIR
    second = (lane % PAIR) >= HALF
    slot = (lane % HALF).astype(jnp.float32)
    gates = gates.astype(jnp.bfloat16).astype(jnp.float32)
    named = jnp.zeros(shape, jnp.float32)
    weight = jnp.zeros(shape, jnp.float32)
    for k in range(picks):
        match = routes[:, k : k + 1] == expert
        named = jnp.where(match, 1.0, named)
        weight = jnp.where(match, gates[:, k : k + 1], weight)
    square = (tok_count, tok_count)
    before = lax.broadcasted_iota(jnp.int32, square, 1) < lax.broadcasted_iota(
        jnp.int32, square, 0
    )
    earlier = dot(jnp.where(before, 1.0, 0.0).astype(jnp.bfloat16), named.astype(jnp.bfloat16))
    hit = jnp.where(earlier == slot, named, 0.0)
    select = jnp.where(second, 0.0, hit).astype(jnp.bfloat16)
    weighting = jnp.where(second, hit * weight, 0.0).astype(jnp.bfloat16)
    return select, weighting


def exchange_kernel(
    n_ctx, n_exp, tokens, cotangent, routes, gates, w_gate_hbm, w_up_hbm, w_down_hbm,
    slots_out, acts_out, back_out, select_out, weighting_out,
    w_gate, w_up, w_down, send, got, total, part, arrived, acts, back_send, back,
    load_sem, out_send, out_recv, sum_send, sum_recv, act_send, act_recv, ret_send, ret_recv,
):
    my_ctx, my_exp = lax.axis_index("ctx"), lax.axis_index("exp")
    width = tokens.shape[1]
    ff = w_gate.shape[1]
    rows = n_exp * HALF
    share = rows // n_ctx
    cuts = pieces(width)

    barrier = pltpu.get_barrier_semaphore()
    for d in range(1, n_exp):
        pl.semaphore_signal(
            barrier, inc=1, device_id=(my_ctx, lax.rem(my_exp + d, n_exp)),
            device_id_type=pl.DeviceIdType.MESH,
        )
    for d in range(1, n_ctx):
        pl.semaphore_signal(
            barrier, inc=1, device_id=(lax.rem(my_ctx + d, n_ctx), my_exp),
            device_id_type=pl.DeviceIdType.MESH,
        )
    loads = [
        pltpu.make_async_copy(src, dst, load_sem.at[i])
        for i, (src, dst) in enumerate(
            ((w_gate_hbm, w_gate), (w_up_hbm, w_up), (w_down_hbm, w_down))
        )
    ]
    for load in loads:
        load.start()

    select, weighting = selections(routes[...], gates[...], n_exp)
    select_out[...] = select
    weighting_out[...] = weighting
    pl.semaphore_wait(barrier, n_exp - 1 + n_ctx - 1)

    def scatter(c, src, dst, send_sem, recv_sem):
        start, size = cuts[c]
        copies = []
        for d in range(1, n_exp):
            peer = lax.rem(my_exp + d, n_exp)
            copy = pltpu.make_async_remote_copy(
                src_ref=src.at[pl.ds(pl.multiple_of(peer * PAIR, PAIR), PAIR), pl.ds(start, size)],
                dst_ref=dst.at[pl.ds(pl.multiple_of(my_exp * PAIR, PAIR), PAIR), pl.ds(start, size)],
                send_sem=send_sem.at[c, d],
                recv_sem=recv_sem.at[c, d],
                device_id=(my_ctx, peer),
                device_id_type=pl.DeviceIdType.MESH,
            )
            copy.start()
            copies.append(copy)
        own = pl.ds(pl.multiple_of(my_exp * PAIR, PAIR), PAIR)
        dst[own, pl.ds(start, size)] = src[own, pl.ds(start, size)]
        return copies

    out_copies = []
    for c, (start, size) in enumerate(cuts):
        cols = pl.ds(start, size)
        send[:, cols] = (
            dot(select, tokens[:, cols], 0, 0) + dot(weighting, cotangent[:, cols], 0, 0)
        ).astype(jnp.bfloat16)
        out_copies.append(scatter(c, send, got, out_send, out_recv))

    my_rows = pl.ds(pl.multiple_of(my_ctx * share, share), share)

    def share_out(index):
        copies = []
        for d in range(1, n_ctx):
            peer = lax.rem(my_ctx + d, n_ctx)
            copy = pltpu.make_async_remote_copy(
                src_ref=part.at[index, pl.ds(pl.multiple_of(peer * share, share), share)],
                dst_ref=arrived.at[index, d],
                send_sem=sum_send.at[index, d],
                recv_sem=sum_recv.at[index, d],
                device_id=(peer, my_exp),
                device_id_type=pl.DeviceIdType.MESH,
            )
            copy.start()
            copies.append(copy)
        return copies

    sum_copies = []
    for c, (start, size) in enumerate(cuts):
        cols = pl.ds(start, size)
        for copy in out_copies[c]:
            copy.wait_recv()
        for index in range(3):
            if c == 0:
                loads[index].wait()
            if index == 0:
                result = dot(got[:, cols], w_gate[cols, :])
            elif index == 1:
                result = dot(got[:, cols], w_up[cols, :])
            else:
                result = dot(got[:, cols], w_down[:, cols], 1, 1)
            result = result.reshape(n_exp, 2, HALF, ff)[:, index // 2].reshape(rows, ff)
            if c:
                result = total[index] + result
            total[index] = result
            if c == len(cuts) - 1:
                part[index] = result.astype(jnp.bfloat16)
                sum_copies.append(share_out(index))
    slots_out[...] = got[...]

    def summed(index):
        result = total[index, my_rows]
        for d in range(1, n_ctx):
            sum_copies[index][d - 1].wait_recv()
            result = result + arrived[index, d].astype(jnp.float32)
        return result

    def gather(index):
        copies = []
        for d in range(1, n_ctx):
            copy = pltpu.make_async_remote_copy(
                src_ref=acts.at[index, my_rows],
                dst_ref=acts.at[index, my_rows],
                send_sem=act_send.at[index, d],
                recv_sem=act_recv.at[index, d],
                device_id=(lax.rem(my_ctx + d, n_ctx), my_exp),
                device_id_type=pl.DeviceIdType.MESH,
            )
            copy.start()
            copies.append(copy)
        return copies

    gate, up = summed(0), summed(1)
    sigmoid = jax.nn.sigmoid(gate)
    activated = gate * sigmoid
    acts[0, my_rows] = (activated * up).astype(jnp.bfloat16)
    act_copies = [gather(0)]
    grad = summed(2)
    acts[1, my_rows] = (grad * up * sigmoid * (1.0 + gate * (1.0 - sigmoid))).astype(jnp.bfloat16)
    act_copies.append(gather(1))
    acts[2, my_rows] = (grad * activated).astype(jnp.bfloat16)
    act_copies.append(gather(2))

    spread = []
    for index in range(3):
        for copy in act_copies[index]:
            copy.wait_recv()
        value = acts[index].astype(jnp.float32).reshape(n_exp, 1, HALF, ff)
        empty = jnp.zeros_like(value)
        both = (empty, value) if index == 0 else (value, empty)
        value = jnp.concatenate(both, axis=1).reshape(n_exp * PAIR, ff).astype(jnp.bfloat16)
        acts_out[index] = value
        spread.append(value)

    ret_copies = []
    for c, (start, size) in enumerate(cuts):
        cols = pl.ds(start, size)
        back_send[:, cols] = (
            dot(spread[0], w_down[:, cols])
            + dot(spread[1], w_gate[cols, :], 1, 1)
            + dot(spread[2], w_up[cols, :], 1, 1)
        ).astype(jnp.bfloat16)
        ret_copies.append(scatter(c, back_send, back, ret_send, ret_recv))
    for c, (start, size) in enumerate(cuts):
        cols = pl.ds(start, size)
        for copy in ret_copies[c]:
            copy.wait_recv()
        back_out[:, cols] = back[:, cols]
    for copies in out_copies + sum_copies + act_copies + ret_copies:
        for copy in copies:
            copy.wait_send()


def gradient_kernel(slots, acts, back, select, weighting, combined, d_tokens, d_gate, d_up, d_down):
    combined[...] = dot(weighting[...], back[...]).astype(jnp.bfloat16)
    d_tokens[...] = dot(select[...], back[...]).astype(jnp.bfloat16)
    d_gate[0] = dot(slots[...], acts[1], 0, 0).astype(jnp.bfloat16)
    d_up[0] = dot(slots[...], acts[2], 0, 0).astype(jnp.bfloat16)
    d_down[0] = dot(acts[0], slots[...], 0, 0).astype(jnp.bfloat16)


def shards(tokens, cotangent, routes, gate_weights, w_gate, w_up, w_down):
    n_ctx, n_exp = lax.axis_size("ctx"), lax.axis_size("exp")
    tok_count, width = tokens.shape
    ff = w_gate.shape[2]
    rows, packed = n_exp * HALF, n_exp * PAIR
    share = rows // n_ctx
    cuts = len(pieces(width))
    bf16, f32 = jnp.bfloat16, jnp.float32
    vmem = pl.BlockSpec(memory_space=pltpu.VMEM)
    hbm = pl.BlockSpec(memory_space=pl.ANY)
    dma = pltpu.SemaphoreType.DMA
    slots, acts, back, select, weighting = pl.pallas_call(
        functools.partial(exchange_kernel, n_ctx, n_exp),
        out_shape=(
            jax.ShapeDtypeStruct((packed, width), bf16),
            jax.ShapeDtypeStruct((3, packed, ff), bf16),
            jax.ShapeDtypeStruct((packed, width), bf16),
            jax.ShapeDtypeStruct((tok_count, packed), bf16),
            jax.ShapeDtypeStruct((tok_count, packed), bf16),
        ),
        in_specs=[vmem] * 4 + [hbm] * 3,
        out_specs=(vmem,) * 5,
        scratch_shapes=[
            pltpu.VMEM((width, ff), bf16),
            pltpu.VMEM((width, ff), bf16),
            pltpu.VMEM((ff, width), bf16),
            pltpu.VMEM((packed, width), bf16),
            pltpu.VMEM((packed, width), bf16),
            pltpu.VMEM((3, rows, ff), f32),
            pltpu.VMEM((3, rows, ff), bf16),
            pltpu.VMEM((3, n_ctx, share, ff), bf16),
            pltpu.VMEM((3, rows, ff), bf16),
            pltpu.VMEM((packed, width), bf16),
            pltpu.VMEM((packed, width), bf16),
            dma((3,)),
            dma((cuts, n_exp)),
            dma((cuts, n_exp)),
            dma((3, n_ctx)),
            dma((3, n_ctx)),
            dma((3, n_ctx)),
            dma((3, n_ctx)),
            dma((cuts, n_exp)),
            dma((cuts, n_exp)),
        ],
        compiler_params=pltpu.CompilerParams(
            collective_id=0, has_side_effects=True, vmem_limit_bytes=44 * 2**20
        ),
    )(tokens, cotangent, routes, gate_weights, w_gate[0], w_up[0], w_down[0])

    block = 256 if width % 256 == 0 else width
    whole = lambda *shape: pl.BlockSpec(shape, lambda i: (0,) * len(shape))
    return pl.pallas_call(
        gradient_kernel,
        grid=(width // block,),
        out_shape=(
            jax.ShapeDtypeStruct((tok_count, width), bf16),
            jax.ShapeDtypeStruct((tok_count, width), bf16),
            jax.ShapeDtypeStruct((1, width, ff), bf16),
            jax.ShapeDtypeStruct((1, width, ff), bf16),
            jax.ShapeDtypeStruct((1, ff, width), bf16),
        ),
        in_specs=[
            pl.BlockSpec((packed, block), lambda i: (0, i)),
            whole(3, packed, ff),
            pl.BlockSpec((packed, block), lambda i: (0, i)),
            whole(tok_count, packed),
            whole(tok_count, packed),
        ],
        out_specs=(
            pl.BlockSpec((tok_count, block), lambda i: (0, i)),
            pl.BlockSpec((tok_count, block), lambda i: (0, i)),
            pl.BlockSpec((1, block, ff), lambda i: (0, i, 0)),
            pl.BlockSpec((1, block, ff), lambda i: (0, i, 0)),
            pl.BlockSpec((1, ff, block), lambda i: (0, 0, i)),
        ),
        compiler_params=pltpu.CompilerParams(vmem_limit_bytes=32 * 2**20),
    )(slots, acts, back, select, weighting)


def solution(mesh):
    in_specs = (
        P("exp", "ctx"),
        P("exp", "ctx"),
        P("exp", None),
        P("exp", None),
        P("exp", "ctx", None),
        P("exp", "ctx", None),
        P("exp", None, "ctx"),
    )
    out_specs = (
        P("exp", "ctx"),
        P("exp", "ctx"),
        P("exp", "ctx", None),
        P("exp", "ctx", None),
        P("exp", None, "ctx"),
    )
    return jax.shard_map(shards, mesh=mesh, in_specs=in_specs, out_specs=out_specs, check_vma=False)
```

time: 127 us -> 57.5 us (0.45)
  Pallas kernels: 0 us -> 48.9 us
  blocking collectives: 45.3 us -> 0 us
  matrix products: 26.8 us -> 0 us
  starting transfers between devices: 25.9 us -> 0 us
  waiting for transfers between devices: 16.5 us -> 0 us
  other arithmetic: 4.15 us -> 0 us
  local copies, waits for them, and re-layouts: 6.08 us -> 7.68 us
    pallas_call x0 -> x2, Pallas kernels: none -> 48.9 us  [the longest x1 42.3 us: shards(): pl.pallas_call(functools.partial(exchange_kernel, n_ctx, n_exp), out_shap...]
    dot_general x13 -> x0, matrix products: 26.8 us -> none  [the longest x5 11.1 us: contract_first(): lax.dot_general(left, right, (((0,), (0,)), ((), ())), preferred_element_...]
    all_gather x3 -> x0, blocking collectives: 25.4 us -> none  [the longest x1 9.5 us: shards(): lax.all_gather(forward_share(gate_sum, up_sum), 'ctx', axis=0, tiled=True)]
    unnamed x1 -> x0, blocking collectives: 19.9 us -> none
    all_to_all x4 -> x0, starting transfers between devices: 18.2 us -> none  [the longest x1 6.33 us: shards(): lax.all_to_all(send_rows.reshape(experts, CAP, feature_width), 'exp', spl...]
    all_to_all x4 -> x0, waiting for transfers between devices: 16.2 us -> none  [the longest x1 6.31 us: shards(): lax.all_to_all(send_rows.reshape(experts, CAP, feature_width), 'exp', spl...]
    unnamed x3 -> x0, starting transfers between devices: 7.7 us -> none
    unnamed x19 -> x10, local copies, waits for them, and re-layouts: 2.24 us -> 7.68 us
  transfers between devices with their start and end apart: 7 -> 0, of which waited for: 4 -> 0; matrix products, arithmetic and copies ran while one was open for 17% -> 0% of each run, Pallas kernels for 0% -> 0%
where the time goes in v1:
time: 57.5 us; the launch traced here: 57.2 us
  Pallas kernels  48.9 us (85%)
  local copies, waits for them, and re-layouts  7.68 us (13%)
  between operations  0.65 us (1%)
    pallas_call x1, Pallas kernels, shards(): pl.pallas_call(functools.partial(exchange_kernel, n_ctx, n_exp), out_shap...  42.3 us
    unnamed x10, local copies, waits for them, and re-layouts  7.68 us
    pallas_call x1, Pallas kernels, shards(): pl.pallas_call(gradient_kernel, grid=(width // block,), out_shape=(jax.Sh...  6.52 us

profile of v1, /device:TPU:0, one launch (start us, length us, event | category | flops | bytes accessed | tf_op | source)
XLA Modules:
  0.0 57.2 jit_solution(10396577865171944711)
XLA Ops:
  0.6 0.8 %copy.12.routes = s32[128,8]{1,0:T(8,128)S(1)} copy(s32[128,8]{0,1:T(8,128)} %param.9) | data formatting | bytes 8192 | tf_op args[2]
  1.4 0.8 %copy.13.gates = f32[128,8]{1,0:T(8,128)S(1)} copy(f32[128,8]{0,1:T(8,128)} %param.10) | data formatting | bytes 8192 | tf_op args[3]
  2.2 0.0 copy-start
  2.2 2.0 %copy-done = bf16[1,1792,1024]{2,1,0:T(8,128)(2,1)S(1)} copy-done((bf16[1,1792,1024]{2,1,0:T(8,128)(2,1)S(1)}, bf16[1,1792,1024]{2,1,0:T(8,128)(2,1)}, u32[]{:S(2)}) %copy-start) | copy-done | bytes 3670040
  4.2 0.0 copy-start.1
  4.2 2.0 %copy-done.1 = bf16[1,1792,1024]{2,1,0:T(8,128)(2,1)S(1)} copy-done((bf16[1,1792,1024]{2,1,0:T(8,128)(2,1)S(1)}, bf16[1,1792,1024]{2,1,0:T(8,128)(2,1)}, u32[]{:S(2)}) %copy-start.1) | copy-done | bytes 3670040
  6.3 0.0 copy-start.2
  6.3 1.0 %copy-done.2 = bf16[128,1792]{1,0:T(8,128)(2,1)S(1)} copy-done((bf16[128,1792]{1,0:T(8,128)(2,1)S(1)}, bf16[128,1792]{1,0:T(8,128)(2,1)}, u32[]{:S(2)}) %copy-start.2) | copy-done | bytes 458776
  7.3 0.0 copy-start.3
  7.3 1.0 %copy-done.3 = bf16[128,1792]{1,0:T(8,128)(2,1)S(1)} copy-done((bf16[128,1792]{1,0:T(8,128)(2,1)S(1)}, bf16[128,1792]{1,0:T(8,128)(2,1)}, u32[]{:S(2)}) %copy-start.3) | copy-done | bytes 458776
  8.3 42.3 %shard_map.110 = (bf16[128,1792]{1,0:T(8,128)(2,1)S(1)}, bf16[3,128,1024]{2,1,0:T(8,128)(2,1)S(1)}, bf16[128,1792]{1,0:T(8,128)(2,1)S(1)}, bf16[128,128]{1,0:T(8,128)(2,1)S(1)}, bf16[128,128]{1,0:T(8,128)(2,1)S(1)}) custom-call(bf16[128,1792]{1,0:T(8,128)(2,1)S(1)} %copy-done.2, bf16[128,1792]{1,0:T(8,128)(2,1)S(1)} %copy-done.3, s32[128,8]{1,0:T(8,128)S(1)} %copy.12.routes, ...), custom_call_target="tpu_custom_call" | custom-call | tf_op jit(solution)/shard_map/pallas_call | solution.py:243
  50.7 6.5 %shard_map.111 = (bf16[128,1792]{1,0:T(8,128)(2,1)}, bf16[128,1792]{1,0:T(8,128)(2,1)}, bf16[1,1792,1024]{2,1,0:T(8,128)(2,1)}, bf16[1,1792,1024]{2,1,0:T(8,128)(2,1)}, bf16[1,1024,1792]{2,1,0:T(8,128)(2,1)}) custom-call(bf16[128,1792]{1,0:T(8,128)(2,1)S(1)} %get-tuple-element.10.slots, bf16[3,128,1024]{2,1,0:T(8,128)(2,1)S(1)} %get-tuple-element.11.acts, ...), custom_call_target="tpu_custom_call" | custom-call | tf_op jit(solution)/shard_map/pallas_call | solution.py:283
Async XLA Ops:
  2.2 2.0 %copy-start = (bf16[1,1792,1024]{2,1,0:T(8,128)(2,1)S(1)}, bf16[1,1792,1024]{2,1,0:T(8,128)(2,1)}, u32[]{:S(2)}) copy-start(bf16[1,1792,1024]{2,1,0:T(8,128)(2,1)} %param.11) | copy-start | bytes 11010052
  4.2 2.0 %copy-start.1 = (bf16[1,1792,1024]{2,1,0:T(8,128)(2,1)S(1)}, bf16[1,1792,1024]{2,1,0:T(8,128)(2,1)}, u32[]{:S(2)}) copy-start(bf16[1,1792,1024]{2,1,0:T(8,128)(2,1)} %param.12) | copy-start | bytes 11010052
  6.3 1.0 %copy-start.2 = (bf16[128,1792]{1,0:T(8,128)(2,1)S(1)}, bf16[128,1792]{1,0:T(8,128)(2,1)}, u32[]{:S(2)}) copy-start(bf16[128,1792]{1,0:T(8,128)(2,1)} %tokens.1) | copy-start | bytes 1376260
  7.3 1.0 %copy-start.3 = (bf16[128,1792]{1,0:T(8,128)(2,1)S(1)}, bf16[128,1792]{1,0:T(8,128)(2,1)}, u32[]{:S(2)}) copy-start(bf16[128,1792]{1,0:T(8,128)(2,1)} %cotangent.1) | copy-start | bytes 1376260

commit v2 on v1

v2 whole, which is shorter than its diff:
```python
import functools

import jax
import jax.numpy as jnp
from jax import lax
from jax.experimental import pallas as pl
from jax.experimental.pallas import tpu as pltpu
from jax.sharding import PartitionSpec as P

HALF = 8
PAIR = 2 * HALF


def dot(left, right, left_dim=1, right_dim=0):
    return lax.dot_general(
        left,
        right,
        (((left_dim,), (right_dim,)), ((), ())),
        preferred_element_type=jnp.float32,
    )


def halves(width):
    first = -(-width // 256) * 128
    return (0, first), (first, width - first)


def widen(value, width):
    if value.shape[1] == width:
        return value
    rest = jnp.zeros((value.shape[0], width - value.shape[1]), value.dtype)
    return jnp.concatenate([value, rest], axis=1)


def selections(routes, gates, count):
    picks, tok_count = routes.shape
    shape = (count * PAIR, tok_count)
    line = lax.broadcasted_iota(jnp.int32, shape, 0)
    expert = line // PAIR
    second = (line % PAIR) >= HALF
    slot = (line % HALF).astype(jnp.float32)
    gates = gates.astype(jnp.bfloat16).astype(jnp.float32)
    named = jnp.zeros(shape, jnp.float32)
    weight = jnp.zeros(shape, jnp.float32)
    for k in range(picks):
        match = routes[k : k + 1, :] == expert
        named = jnp.where(match, 1.0, named)
        weight = jnp.where(match, gates[k : k + 1, :], weight)
    square = (tok_count, tok_count)
    before = lax.broadcasted_iota(jnp.int32, square, 0) < lax.broadcasted_iota(
        jnp.int32, square, 1
    )
    earlier = dot(named.astype(jnp.bfloat16), jnp.where(before, 1.0, 0.0).astype(jnp.bfloat16))
    hit = jnp.where(earlier == slot, named, 0.0)
    weight = hit * weight
    return [
        jnp.where(second == later, value, 0.0).astype(jnp.bfloat16)
        for value in (hit, weight)
        for later in (False, True)
    ]


def exchange_kernel(
    n_ctx, n_exp, routes, gates, tokens_hbm, cotangent_hbm, w_gate_hbm, w_up_hbm, w_down_hbm,
    slots_out, acts_out, back_out, select_out,
    tokens, cotangent, w_gate, w_up, w_down, send, got, total, part, arrived, acts, back_send, back,
    load_sem, out_send, out_recv, sum_send, sum_recv, act_send, act_recv, ret_send, ret_recv,
):
    my_ctx, my_exp = lax.axis_index("ctx"), lax.axis_index("exp")
    width = tokens.shape[1]
    ff = w_gate.shape[1]
    rows = n_exp * HALF
    share = rows // n_ctx
    left, right = halves(width)
    left, right, half = pl.ds(*left), pl.ds(*right), left[1]

    barrier = pltpu.get_barrier_semaphore()
    for d in range(1, n_exp):
        pl.semaphore_signal(
            barrier, inc=1, device_id=(my_ctx, lax.rem(my_exp + d, n_exp)),
            device_id_type=pl.DeviceIdType.MESH,
        )
    for d in range(1, n_ctx):
        pl.semaphore_signal(
            barrier, inc=1, device_id=(lax.rem(my_ctx + d, n_ctx), my_exp),
            device_id_type=pl.DeviceIdType.MESH,
        )
    loads = [
        pltpu.make_async_copy(src, dst, load_sem.at[i])
        for i, (src, dst) in enumerate(
            (
                (tokens_hbm, tokens),
                (cotangent_hbm, cotangent),
                (w_gate_hbm, w_gate),
                (w_up_hbm, w_up),
                (w_down_hbm, w_down),
            )
        )
    ]
    for load in loads:
        load.start()

    chosen = selections(routes[...], gates[...], n_exp)

    def scatter(kind, src, dst, send_sem, recv_sem):
        copies = []
        mine = pl.ds(pl.multiple_of(my_exp * PAIR, PAIR), PAIR)
        for d in range(1, n_exp):
            peer = lax.rem(my_exp + d, n_exp)
            copy = pltpu.make_async_remote_copy(
                src_ref=src.at[kind, pl.ds(pl.multiple_of(peer * PAIR, PAIR), PAIR)],
                dst_ref=dst.at[kind, mine],
                send_sem=send_sem.at[kind, d],
                recv_sem=recv_sem.at[kind, d],
                device_id=(my_ctx, peer),
                device_id_type=pl.DeviceIdType.MESH,
            )
            copy.start()
            copies.append(copy)
        dst[kind, mine] = src[kind, mine]
        return copies

    out_copies = []
    for kind, data in enumerate((tokens, cotangent)):
        loads[kind].wait()
        send[kind] = (
            dot(chosen[2 * kind], data[:, left])
            + widen(dot(chosen[2 * kind + 1], data[:, right]), half)
        ).astype(jnp.bfloat16)
        if kind == 0:
            pl.semaphore_wait(barrier, n_exp - 1 + n_ctx - 1)
        out_copies.append(scatter(kind, send, got, out_send, out_recv))
    for i in range(4):
        select_out[i] = chosen[i]

    my_rows = pl.ds(pl.multiple_of(my_ctx * share, share), share)

    def share_out(index):
        copies = []
        for d in range(1, n_ctx):
            peer = lax.rem(my_ctx + d, n_ctx)
            copy = pltpu.make_async_remote_copy(
                src_ref=part.at[index, pl.ds(pl.multiple_of(peer * share, share), share)],
                dst_ref=arrived.at[index, d],
                send_sem=sum_send.at[index, d],
                recv_sem=sum_recv.at[index, d],
                device_id=(peer, my_exp),
                device_id_type=pl.DeviceIdType.MESH,
            )
            copy.start()
            copies.append(copy)
        return copies

    def pick(value, which):
        return value.reshape(n_exp, 2, HALF, ff)[:, which].reshape(rows, ff)

    sum_copies = []
    for index in range(3):
        kind = index // 2
        if index != 1:
            for copy in out_copies[kind]:
                copy.wait_recv()
        loads[2 + index].wait()
        rest = pl.ds(0, right.size)
        if index < 2:
            weights = w_gate if index == 0 else w_up
            first = dot(got[kind], weights[left, :])
            second = dot(got[kind, :, rest], weights[right, :])
        else:
            first = dot(got[kind], w_down[:, left], 1, 1)
            second = dot(got[kind, :, rest], w_down[:, right], 1, 1)
        result = pick(first, 0) + pick(second, 1)
        total[index] = result
        part[index] = result.astype(jnp.bfloat16)
        sum_copies.append(share_out(index))
    slots_out[...] = got[...]

    def summed(index):
        result = total[index, my_rows]
        for d in range(1, n_ctx):
            sum_copies[index][d - 1].wait_recv()
            result = result + arrived[index, d].astype(jnp.float32)
        return result

    def gather(index):
        copies = []
        for d in range(1, n_ctx):
            copy = pltpu.make_async_remote_copy(
                src_ref=acts.at[index, my_rows],
                dst_ref=acts.at[index, my_rows],
                send_sem=act_send.at[index, d],
                recv_sem=act_recv.at[index, d],
                device_id=(lax.rem(my_ctx + d, n_ctx), my_exp),
                device_id_type=pl.DeviceIdType.MESH,
            )
            copy.start()
            copies.append(copy)
        return copies

    gate, up = summed(0), summed(1)
    sigmoid = jax.nn.sigmoid(gate)
    activated = gate * sigmoid
    acts[0, my_rows] = (activated * up).astype(jnp.bfloat16)
    act_copies = [gather(0)]
    grad = summed(2)
    acts[1, my_rows] = (grad * up * sigmoid * (1.0 + gate * (1.0 - sigmoid))).astype(jnp.bfloat16)
    act_copies.append(gather(1))
    acts[2, my_rows] = (grad * activated).astype(jnp.bfloat16)
    act_copies.append(gather(2))

    def pack(first, second):
        both = [first, widen(second, half)]
        both = [value.reshape(n_exp, 1, HALF, half) for value in both]
        return jnp.concatenate(both, axis=1).reshape(n_exp * PAIR, half).astype(jnp.bfloat16)

    for copy in act_copies[0]:
        copy.wait_recv()
    back_send[0] = pack(dot(acts[0], w_down[:, left]), dot(acts[0], w_down[:, right]))
    ret_copies = [scatter(0, back_send, back, ret_send, ret_recv)]
    for copy in act_copies[1] + act_copies[2]:
        copy.wait_recv()
    back_send[1] = pack(
        dot(acts[1], w_gate[left, :], 1, 1) + dot(acts[2], w_up[left, :], 1, 1),
        dot(acts[1], w_gate[right, :], 1, 1) + dot(acts[2], w_up[right, :], 1, 1),
    )
    ret_copies.append(scatter(1, back_send, back, ret_send, ret_recv))
    acts_out[...] = acts[...]
    for kind in range(2):
        for copy in ret_copies[kind]:
            copy.wait_recv()
        back_out[kind] = back[kind]
    for copies in out_copies + sum_copies + act_copies + ret_copies:
        for copy in copies:
            copy.wait_send()


def gradient_kernel(
    n_exp, slots, acts, back, select, combined_hbm, d_tokens_hbm, d_gate_hbm, d_up_hbm, d_down_hbm,
    combined, d_tokens, d_gate, d_up, d_down, sems,
):
    width, ff = d_gate.shape
    rows = n_exp * HALF
    cuts = halves(width)
    copies = []

    def store(src, dst):
        copy = pltpu.make_async_copy(src, dst, sems.at[len(copies)])
        copy.start()
        copies.append(copy)

    def unpack(kind):
        value = slots[kind].astype(jnp.float32).reshape(n_exp, 2, HALF, -1)
        return [
            value[:, i].reshape(rows, -1)[:, :size].astype(jnp.bfloat16)
            for i, (_, size) in enumerate(cuts)
        ]

    row_halves = unpack(0)
    for i, (start, size) in enumerate(cuts):
        at = pl.ds(start, size)
        for index, buf, hbm in ((1, d_gate, d_gate_hbm), (2, d_up, d_up_hbm)):
            buf[at, :] = dot(row_halves[i], acts[index], 0, 0).astype(jnp.bfloat16)
            store(buf.at[at], hbm.at[at])
    grad_halves = unpack(1)
    for lo in range(0, ff, ff // 2):
        at = pl.ds(lo, ff // 2)
        for i, (start, size) in enumerate(cuts):
            d_down[at, pl.ds(start, size)] = dot(acts[0, :, at], grad_halves[i], 0, 0).astype(
                jnp.bfloat16
            )
        store(d_down.at[at], d_down_hbm.at[at])
    for kind, buf, hbm in ((0, combined, combined_hbm), (1, d_tokens, d_tokens_hbm)):
        for i, (start, size) in enumerate(cuts):
            matrix = select[2 * (1 - kind) + i]
            buf[:, pl.ds(start, size)] = dot(matrix, back[kind, :, pl.ds(0, size)], 0, 0).astype(
                jnp.bfloat16
            )
        store(buf, hbm)
    for copy in copies:
        copy.wait()


def shards(tokens, cotangent, routes, gate_weights, w_gate, w_up, w_down):
    n_ctx, n_exp = lax.axis_size("ctx"), lax.axis_size("exp")
    tok_count, width = tokens.shape
    ff = w_gate.shape[2]
    rows, packed = n_exp * HALF, n_exp * PAIR
    share = rows // n_ctx
    half = halves(width)[0][1]
    bf16, f32 = jnp.bfloat16, jnp.float32
    vmem = pl.BlockSpec(memory_space=pltpu.VMEM)
    hbm = pl.BlockSpec(memory_space=pltpu.HBM)
    dma = pltpu.SemaphoreType.DMA
    slots, acts, back, select = pl.pallas_call(
        functools.partial(exchange_kernel, n_ctx, n_exp),
        out_shape=(
            jax.ShapeDtypeStruct((2, packed, half), bf16),
            jax.ShapeDtypeStruct((3, rows, ff), bf16),
            jax.ShapeDtypeStruct((2, packed, half), bf16),
            jax.ShapeDtypeStruct((4, packed, tok_count), bf16),
        ),
        in_specs=[vmem] * 2 + [hbm] * 5,
        out_specs=(vmem,) * 4,
        scratch_shapes=[
            pltpu.VMEM((tok_count, width), bf16),
            pltpu.VMEM((tok_count, width), bf16),
            pltpu.VMEM((width, ff), bf16),
            pltpu.VMEM((width, ff), bf16),
            pltpu.VMEM((ff, width), bf16),
            pltpu.VMEM((2, packed, half), bf16),
            pltpu.VMEM((2, packed, half), bf16),
            pltpu.VMEM((3, rows, ff), f32),
            pltpu.VMEM((3, rows, ff), bf16),
            pltpu.VMEM((3, n_ctx, share, ff), bf16),
            pltpu.VMEM((3, rows, ff), bf16),
            pltpu.VMEM((2, packed, half), bf16),
            pltpu.VMEM((2, packed, half), bf16),
            dma((5,)),
            dma((2, n_exp)),
            dma((2, n_exp)),
            dma((3, n_ctx)),
            dma((3, n_ctx)),
            dma((3, n_ctx)),
            dma((3, n_ctx)),
            dma((2, n_exp)),
            dma((2, n_exp)),
        ],
        compiler_params=pltpu.CompilerParams(
            collective_id=0, has_side_effects=True, vmem_limit_bytes=60 * 2**20
        ),
    )(routes.T, gate_weights.T, tokens, cotangent, w_gate[0], w_up[0], w_down[0])

    combined, d_tokens, d_gate, d_up, d_down = pl.pallas_call(
        functools.partial(gradient_kernel, n_exp),
        out_shape=(
            jax.ShapeDtypeStruct((tok_count, width), bf16),
            jax.ShapeDtypeStruct((tok_count, width), bf16),
            jax.ShapeDtypeStruct((width, ff), bf16),
            jax.ShapeDtypeStruct((width, ff), bf16),
            jax.ShapeDtypeStruct((ff, width), bf16),
        ),
        in_specs=[vmem] * 4,
        out_specs=(hbm,) * 5,
        scratch_shapes=[
            pltpu.VMEM((tok_count, width), bf16),
            pltpu.VMEM((tok_count, width), bf16),
            pltpu.VMEM((width, ff), bf16),
            pltpu.VMEM((width, ff), bf16),
            pltpu.VMEM((ff, width), bf16),
            dma((8,)),
        ],
        compiler_params=pltpu.CompilerParams(vmem_limit_bytes=44 * 2**20),
    )(slots, acts, back, select)
    return combined, d_tokens, d_gate[None], d_up[None], d_down[None]


def solution(mesh):
    in_specs = (
        P("exp", "ctx"),
        P("exp", "ctx"),
        P("exp", None),
        P("exp", None),
        P("exp", "ctx", None),
        P("exp", "ctx", None),
        P("exp", None, "ctx"),
    )
    out_specs = (
        P("exp", "ctx"),
        P("exp", "ctx"),
        P("exp", "ctx", None),
        P("exp", "ctx", None),
        P("exp", None, "ctx"),
    )
    return jax.shard_map(shards, mesh=mesh, in_specs=in_specs, out_specs=out_specs, check_vma=False)
```

time: 57.5 us -> 47 us (0.82)
  Pallas kernels: 48.9 us -> 41.6 us
  local copies, waits for them, and re-layouts: 7.68 us -> 3.93 us
    pallas_call x1, Pallas kernels: 42.3 us -> 36.5 us  [shards(): pl.pallas_call(functools.partial(exchange_kernel, n_ctx, n_exp), out_shap...]
    unnamed x10 -> x8, local copies, waits for them, and re-layouts: 7.68 us -> 3.93 us
    pallas_call x1, Pallas kernels: 6.52 us -> 5.1 us  [shards(): pl.pallas_call(functools.partial(gradient_kernel, n_exp), out_shape=(jax....]
where the time goes in v2:
time: 47 us; the launch traced here: 46.2 us
  Pallas kernels  41.6 us (89%)
  local copies, waits for them, and re-layouts  3.93 us (8%)
  between operations  0.65 us (1%)
    pallas_call x1, Pallas kernels, shards(): pl.pallas_call(functools.partial(exchange_kernel, n_ctx, n_exp), out_shap...  36.5 us
    pallas_call x1, Pallas kernels, shards(): pl.pallas_call(functools.partial(gradient_kernel, n_exp), out_shape=(jax....  5.1 us
    unnamed x8, local copies, waits for them, and re-layouts  3.93 us

profile of v2, /device:TPU:0, one launch (start us, length us, event | category | flops | bytes accessed | tf_op | source)
XLA Modules:
  0.0 46.2 jit_solution(3093917832810391217)
XLA Ops:
  0.6 36.5 %shard_map.110 = (bf16[2,128,896]{2,1,0:T(8,128)(2,1)}, bf16[3,64,1024]{2,1,0:T(8,128)(2,1)}, bf16[2,128,896]{2,1,0:T(8,128)(2,1)}, bf16[4,128,128]{2,1,0:T(8,128)(2,1)}) custom-call(s32[8,128]{1,0:T(8,128)} %bitcast.11, f32[8,128]{1,0:T(8,128)} %bitcast.12, bf16[128,1792]{1,0:T(8,128)(2,1)} %tokens_hbm.1, bf16[128,1792]{1,0:T(8,128)(2,1)} %cotangent_hbm.1, ...), custom_call_target="tpu_custom_call" | custom-call | tf_op jit(solution)/shard_map/pallas_call | solution.py:294
  37.2 0.0 copy-start
  37.2 1.0 %copy-done = bf16[2,128,896]{2,1,0:T(8,128)(2,1)S(1)} copy-done((bf16[2,128,896]{2,1,0:T(8,128)(2,1)S(1)}, bf16[2,128,896]{2,1,0:T(8,128)(2,1)}, u32[]{:S(2)}) %copy-start) | copy-done | bytes 458776
  38.2 0.0 copy-start.1
  38.2 1.0 %copy-done.1 = bf16[2,128,896]{2,1,0:T(8,128)(2,1)S(1)} copy-done((bf16[2,128,896]{2,1,0:T(8,128)(2,1)S(1)}, bf16[2,128,896]{2,1,0:T(8,128)(2,1)}, u32[]{:S(2)}) %copy-start.1) | copy-done | bytes 458776
  39.2 0.0 copy-start.2
  39.2 1.0 %copy-done.2 = bf16[3,64,1024]{2,1,0:T(8,128)(2,1)S(1)} copy-done((bf16[3,64,1024]{2,1,0:T(8,128)(2,1)S(1)}, bf16[3,64,1024]{2,1,0:T(8,128)(2,1)}, u32[]{:S(2)}) %copy-start.2) | copy-done | bytes 393240
  40.2 0.0 copy-start.3
  40.2 0.9 %copy-done.3 = bf16[4,128,128]{2,1,0:T(8,128)(2,1)S(1)} copy-done((bf16[4,128,128]{2,1,0:T(8,128)(2,1)S(1)}, bf16[4,128,128]{2,1,0:T(8,128)(2,1)}, u32[]{:S(2)}) %copy-start.3) | copy-done | bytes 131096
  41.1 5.1 %shard_map.111 = (bf16[128,1792]{1,0:T(8,128)(2,1)}, bf16[128,1792]{1,0:T(8,128)(2,1)}, bf16[1792,1024]{1,0:T(8,128)(2,1)}, bf16[1792,1024]{1,0:T(8,128)(2,1)}, bf16[1024,1792]{1,0:T(8,128)(2,1)}) custom-call(bf16[2,128,896]{2,1,0:T(8,128)(2,1)S(1)} %copy-done, bf16[3,64,1024]{2,1,0:T(8,128)(2,1)S(1)} %copy-done.2, bf16[2,128,896]{2,1,0:T(8,128)(2,1)S(1)} %copy-done.1, ...), custom_call_target="tpu_custom_call" | custom-call | tf_op jit(solution)/shard_map/pallas_call | solution.py:333
Async XLA Ops:
  37.2 1.0 %copy-start = (bf16[2,128,896]{2,1,0:T(8,128)(2,1)S(1)}, bf16[2,128,896]{2,1,0:T(8,128)(2,1)}, u32[]{:S(2)}) copy-start(bf16[2,128,896]{2,1,0:T(8,128)(2,1)} %get-tuple-element.14.slots) | copy-start | bytes 1376260
  38.2 1.0 %copy-start.1 = (bf16[2,128,896]{2,1,0:T(8,128)(2,1)S(1)}, bf16[2,128,896]{2,1,0:T(8,128)(2,1)}, u32[]{:S(2)}) copy-start(bf16[2,128,896]{2,1,0:T(8,128)(2,1)} %get-tuple-element.16.back) | copy-start | bytes 1376260
  39.2 1.0 %copy-start.2 = (bf16[3,64,1024]{2,1,0:T(8,128)(2,1)S(1)}, bf16[3,64,1024]{2,1,0:T(8,128)(2,1)}, u32[]{:S(2)}) copy-start(bf16[3,64,1024]{2,1,0:T(8,128)(2,1)} %get-tuple-element.15.acts) | copy-start | bytes 1179652
  40.2 0.9 %copy-start.3 = (bf16[4,128,128]{2,1,0:T(8,128)(2,1)S(1)}, bf16[4,128,128]{2,1,0:T(8,128)(2,1)}, u32[]{:S(2)}) copy-start(bf16[4,128,128]{2,1,0:T(8,128)(2,1)} %get-tuple-element.17.select) | copy-start | bytes 393220

commit v3 on v2

--- a/solution.py
+++ b/solution.py
@@ -63,8 +63,8 @@
 def exchange_kernel(
     n_ctx, n_exp, routes, gates, tokens_hbm, cotangent_hbm, w_gate_hbm, w_up_hbm, w_down_hbm,
     slots_out, acts_out, back_out, select_out,
-    tokens, cotangent, w_gate, w_up, w_down, send, got, total, part, arrived, acts, back_send, back,
-    load_sem, out_send, out_recv, sum_send, sum_recv, act_send, act_recv, ret_send, ret_recv,
+    tokens, cotangent, w_gate, w_up, w_down, select, send, got, total, part, arrived, acts, back_send,
+    back, load_sem, store_sem, out_send, out_recv, sum_send, sum_recv, act_send, act_recv, ret_send, ret_recv,
 ):
     my_ctx, my_exp = lax.axis_index("ctx"), lax.axis_index("exp")
     width = tokens.shape[1]
@@ -130,8 +130,16 @@
         if kind == 0:
             pl.semaphore_wait(barrier, n_exp - 1 + n_ctx - 1)
         out_copies.append(scatter(kind, send, got, out_send, out_recv))
+    stores = []
+
+    def store(src, dst):
+        copy = pltpu.make_async_copy(src, dst, store_sem.at[len(stores)])
+        copy.start()
+        stores.append(copy)
+
     for i in range(4):
-        select_out[i] = chosen[i]
+        select[i] = chosen[i]
+    store(select, select_out)
 
     my_rows = pl.ds(pl.multiple_of(my_ctx * share, share), share)
 
@@ -173,7 +181,7 @@
         total[index] = result
         part[index] = result.astype(jnp.bfloat16)
         sum_copies.append(share_out(index))
-    slots_out[...] = got[...]
+    store(got, slots_out)
 
     def summed(index):
         result = total[index, my_rows]
@@ -217,27 +225,41 @@
         copy.wait_recv()
     back_send[0] = pack(dot(acts[0], w_down[:, left]), dot(acts[0], w_down[:, right]))
     ret_copies = [scatter(0, back_send, back, ret_send, ret_recv)]
-    for copy in act_copies[1] + act_copies[2]:
+    for copy in act_copies[1]:
+        copy.wait_recv()
+    first, second = dot(acts[1], w_gate[left, :], 1, 1), dot(acts[1], w_gate[right, :], 1, 1)
+    for copy in act_copies[2]:
         copy.wait_recv()
     back_send[1] = pack(
-        dot(acts[1], w_gate[left, :], 1, 1) + dot(acts[2], w_up[left, :], 1, 1),
-        dot(acts[1], w_gate[right, :], 1, 1) + dot(acts[2], w_up[right, :], 1, 1),
+        first + dot(acts[2], w_up[left, :], 1, 1),
+        second + dot(acts[2], w_up[right, :], 1, 1),
     )
     ret_copies.append(scatter(1, back_send, back, ret_send, ret_recv))
-    acts_out[...] = acts[...]
+    store(acts, acts_out)
     for kind in range(2):
         for copy in ret_copies[kind]:
             copy.wait_recv()
-        back_out[kind] = back[kind]
+        store(back.at[kind], back_out.at[kind])
     for copies in out_copies + sum_copies + act_copies + ret_copies:
         for copy in copies:
             copy.wait_send()
+    for copy in stores:
+        copy.wait()
 
 
 def gradient_kernel(
-    n_exp, slots, acts, back, select, combined_hbm, d_tokens_hbm, d_gate_hbm, d_up_hbm, d_down_hbm,
-    combined, d_tokens, d_gate, d_up, d_down, sems,
+    n_exp, slots_hbm, acts_hbm, back_hbm, select_hbm,
+    combined_hbm, d_tokens_hbm, d_gate_hbm, d_up_hbm, d_down_hbm,
+    slots, acts, back, select, combined, d_tokens, d_gate, d_up, d_down, load_sem, sems,
 ):
+    loads = [
+        pltpu.make_async_copy(src, dst, load_sem.at[i])
+        for i, (src, dst) in enumerate(
+            ((slots_hbm, slots), (acts_hbm, acts), (back_hbm, back), (select_hbm, select))
+        )
+    ]
+    for load in loads:
+        load.start()
     width, ff = d_gate.shape
     rows = n_exp * HALF
     cuts = halves(width)
@@ -255,7 +277,9 @@
             for i, (_, size) in enumerate(cuts)
         ]
 
+    loads[0].wait()
     row_halves = unpack(0)
+    loads[1].wait()
     for i, (start, size) in enumerate(cuts):
         at = pl.ds(start, size)
         for index, buf, hbm in ((1, d_gate, d_gate_hbm), (2, d_up, d_up_hbm)):
@@ -269,6 +293,8 @@
                 jnp.bfloat16
             )
         store(d_down.at[at], d_down_hbm.at[at])
+    loads[2].wait()
+    loads[3].wait()
     for kind, buf, hbm in ((0, combined, combined_hbm), (1, d_tokens, d_tokens_hbm)):
         for i, (start, size) in enumerate(cuts):
             matrix = select[2 * (1 - kind) + i]
@@ -300,13 +326,14 @@
             jax.ShapeDtypeStruct((4, packed, tok_count), bf16),
         ),
         in_specs=[vmem] * 2 + [hbm] * 5,
-        out_specs=(vmem,) * 4,
+        out_specs=(hbm,) * 4,
         scratch_shapes=[
             pltpu.VMEM((tok_count, width), bf16),
             pltpu.VMEM((tok_count, width), bf16),
             pltpu.VMEM((width, ff), bf16),
             pltpu.VMEM((width, ff), bf16),
             pltpu.VMEM((ff, width), bf16),
+            pltpu.VMEM((4, packed, tok_count), bf16),
             pltpu.VMEM((2, packed, half), bf16),
             pltpu.VMEM((2, packed, half), bf16),
             pltpu.VMEM((3, rows, ff), f32),
@@ -315,6 +342,7 @@
             pltpu.VMEM((3, rows, ff), bf16),
             pltpu.VMEM((2, packed, half), bf16),
             pltpu.VMEM((2, packed, half), bf16),
+            dma((5,)),
             dma((5,)),
             dma((2, n_exp)),
             dma((2, n_exp)),
@@ -339,17 +367,22 @@
             jax.ShapeDtypeStruct((width, ff), bf16),
             jax.ShapeDtypeStruct((ff, width), bf16),
         ),
-        in_specs=[vmem] * 4,
+        in_specs=[hbm] * 4,
         out_specs=(hbm,) * 5,
         scratch_shapes=[
+            pltpu.VMEM((2, packed, half), bf16),
+            pltpu.VMEM((3, rows, ff), bf16),
+            pltpu.VMEM((2, packed, half), bf16),
+            pltpu.VMEM((4, packed, tok_count), bf16),
             pltpu.VMEM((tok_count, width), bf16),
             pltpu.VMEM((tok_count, width), bf16),
             pltpu.VMEM((width, ff), bf16),
             pltpu.VMEM((width, ff), bf16),
             pltpu.VMEM((ff, width), bf16),
+            dma((4,)),
             dma((8,)),
         ],
-        compiler_params=pltpu.CompilerParams(vmem_limit_bytes=44 * 2**20),
+        compiler_params=pltpu.CompilerParams(vmem_limit_bytes=60 * 2**20),
     )(slots, acts, back, select)
     return combined, d_tokens, d_gate[None], d_up[None], d_down[None]
 

time: 47 us -> 43.6 us (0.928)
  local copies, waits for them, and re-layouts: 3.93 us -> 0 us
  Pallas kernels: 41.6 us -> 42.3 us
    unnamed x8 -> x0, local copies, waits for them, and re-layouts: 3.93 us -> none
    pallas_call x1, Pallas kernels: 5.1 us -> 6.29 us  [shards(): pl.pallas_call(functools.partial(gradient_kernel, n_exp), out_shape=(jax....]
    pallas_call x1, Pallas kernels: 36.5 us -> 36 us  [shards(): pl.pallas_call(functools.partial(exchange_kernel, n_ctx, n_exp), out_shap...]
where the time goes in v3:
time: 43.6 us; the launch traced here: 43 us
  Pallas kernels  42.3 us (97%)
  between operations  0.64 us (1%)
    pallas_call x1, Pallas kernels, shards(): pl.pallas_call(functools.partial(exchange_kernel, n_ctx, n_exp), out_shap...  36 us
    pallas_call x1, Pallas kernels, shards(): pl.pallas_call(functools.partial(gradient_kernel, n_exp), out_shape=(jax....  6.29 us

profile of v3, /device:TPU:0, one launch (start us, length us, event | category | flops | bytes accessed | tf_op | source)
XLA Modules:
  0.0 43.0 jit_solution(17482909853692560665)
XLA Ops:
  0.6 36.0 %shard_map.110 = (bf16[2,128,896]{2,1,0:T(8,128)(2,1)}, bf16[3,64,1024]{2,1,0:T(8,128)(2,1)}, bf16[2,128,896]{2,1,0:T(8,128)(2,1)}, bf16[4,128,128]{2,1,0:T(8,128)(2,1)}) custom-call(s32[8,128]{1,0:T(8,128)} %bitcast.11, f32[8,128]{1,0:T(8,128)} %bitcast.12, bf16[128,1792]{1,0:T(8,128)(2,1)} %tokens_hbm.1, bf16[128,1792]{1,0:T(8,128)(2,1)} %cotangent_hbm.1, ...), custom_call_target="tpu_custom_call" | custom-call | tf_op jit(solution)/shard_map/pallas_call | solution.py:320
  36.7 6.3 %shard_map.111 = (bf16[128,1792]{1,0:T(8,128)(2,1)}, bf16[128,1792]{1,0:T(8,128)(2,1)}, bf16[1792,1024]{1,0:T(8,128)(2,1)}, bf16[1792,1024]{1,0:T(8,128)(2,1)}, bf16[1024,1792]{1,0:T(8,128)(2,1)}) custom-call(bf16[2,128,896]{2,1,0:T(8,128)(2,1)} %get-tuple-element.14.slots_hbm, bf16[3,64,1024]{2,1,0:T(8,128)(2,1)} %get-tuple-element.15.acts_hbm, ...), custom_call_target="tpu_custom_call" | custom-call | tf_op jit(solution)/shard_map/pallas_call | solution.py:361
